TPU v7x, 32 devices: a whole 2x2x4 slice. The times are simulated.
32 devices in a mesh: sector: 8 (over z, y), mpo: 4 (over x, core).
Axes of the slice: x: 2, y: 2, z: 4, core: 2. Of those that a mesh axis runs over, the one named last changes fastest.
Arguments:
- psi: bfloat16 [16, 128, 2048], P('sector', 'mpo'), may hold values from -150 to 150
- left_env: bfloat16 [16, 128, 128, 128], P('sector', 'mpo'), may hold values from -0.5 to 0.5
- right_env: bfloat16 [16, 128, 128, 128], P('sector', 'mpo'), may hold values from -0.046875 to 0.046875
- term_op: int32 [128], P('mpo'), may hold values from 0 to 7
- ops: bfloat16 [8, 16, 16], replicated, may hold values from -1.5 to 1.5
- energy: float32 [16], replicated, may hold values from -2 to 2
- charge: int32 [16], P('sector'), may hold values from 0 to 15
- block_dims: int32 [16, 2], P('sector'), may hold values from 64 to 128, as said below
- basis: float32 [3, 16, 128, 2048], P(None, 'sector', 'mpo'), may hold values from -0.0029296875 to 0.0029296875
Outputs:
- hpsi: float32 [16, 128, 2048], P('sector', 'mpo')
- correction: float32 [16, 128, 2048], P('sector', 'mpo')
- ritz: float32 [], replicated
- subspace_row: float32 [3], replicated
Inputs may be any that keep to these rules, and one draw needn't show every extreme that they name: block_dims[s, 0] rows and block_dims[s, 1] columns of each padded block are valid; some block is full.
All inputs are finite; a program needn't handle non-finite values.
Results may differ from a plain program's by a relative error of at most 0.002.
Values may be sent and summed in bfloat16 or wider, within the bound.
A program may use at most 64 MiB of HBM per device.

v0:
```python
import functools

import jax
import jax.numpy as jnp
from jax import lax
from jax.experimental import pallas as pl
from jax.experimental.pallas import tpu as pltpu
from jax.sharding import PartitionSpec as P

MESH = pl.DeviceIdType.MESH


def gather_kernel(n, sectors, flat, psi_ref, out_ref, own_sem, send, recv, fsend, frecv):
    row = lax.axis_index("sector")
    me = lax.axis_index("mpo")
    chips = n // 2
    core, chip = lax.rem(me, 2), lax.div(me, 2)
    sib = chip * 2 + 1 - core

    rows = psi_ref.shape[1]

    def at(hop):
        return lax.rem(chip + hop, chips) * 2

    def slot(block, s):
        if flat:
            return out_ref.at[s, pl.ds(pl.multiple_of(block * rows, rows), rows)]
        return out_ref.at[block, s]

    barrier = pltpu.get_barrier_semaphore()
    for hop in range(1, chips):
        pl.semaphore_signal(barrier, inc=1, device_id=(row, at(hop) + core), device_id_type=MESH)
    pl.semaphore_signal(barrier, inc=1, device_id=(row, sib), device_id_type=MESH)
    pl.semaphore_wait(barrier, chips)

    def push(src, block, s, to, ssem, rsem):
        return pltpu.make_async_remote_copy(
            src_ref=src,
            dst_ref=slot(block, s),
            send_sem=ssem,
            recv_sem=rsem,
            device_id=(row, to),
            device_id_type=MESH,
        )

    far, near, relay = {}, {}, {}
    for s in range(sectors):
        for hop in range(1, chips):
            far[hop, s] = push(
                psi_ref.at[s], me, s, at(hop) + core, send.at[hop, s], recv.at[hop, s]
            )
            far[hop, s].start()
    for s in range(sectors):
        near[s] = push(psi_ref.at[s], me, s, sib, send.at[0, s], recv.at[0, s])
        near[s].start()
    own = [
        pltpu.make_async_copy(psi_ref.at[s], slot(me, s), own_sem.at[s]) for s in range(sectors)
    ]
    for copy in own:
        copy.start()
    for s in range(sectors):
        for hop in range(1, chips):
            far[hop, s].wait_recv()
            block = at(chips - hop) + core
            relay[hop, s] = push(
                slot(block, s), block, s, sib, fsend.at[hop, s], frecv.at[hop, s]
            )
            relay[hop, s].start()
    for s in range(sectors):
        own[s].wait()
        near[s].wait()
        for hop in range(1, chips):
            far[hop, s].wait_send()
            relay[hop, s].wait()


def gather(psi, n):
    sectors, rows, width = psi.shape
    chips = n // 2
    flat = rows % 16 == 0
    shape = (sectors, n * rows, width) if flat else (n, sectors, rows, width)
    out = pl.pallas_call(
        functools.partial(gather_kernel, n, sectors, flat),
        out_shape=jax.ShapeDtypeStruct(shape, psi.dtype),
        in_specs=[pl.BlockSpec(memory_space=pl.ANY)],
        out_specs=pl.BlockSpec(memory_space=pl.ANY),
        scratch_shapes=[pltpu.SemaphoreType.DMA((sectors,))]
        + [pltpu.SemaphoreType.DMA((chips, sectors))] * 4,
        compiler_params=pltpu.CompilerParams(collective_id=0, has_side_effects=True),
        name="gather",
    )(psi)
    if flat:
        return out
    return jnp.transpose(out, (1, 0, 2, 3)).reshape(sectors, n * rows, width)


def terms_kernel(
    size_p, op_ref, opmat_ref, x_ref, left_ref, right_ref, out_ref, sums, count, first, lists
):
    terms = left_ref.shape[1]
    blk = left_ref.shape[2]
    op_count = count.shape[0]
    slots = lists.shape[1]
    pitch = sums.shape[1] // size_p

    for o in range(op_count):
        count[o] = 0

    def tally(k, c):
        o = op_ref[k]
        count[o] = count[o] + 1
        return c

    lax.fori_loop(0, terms, tally, 0)
    total = jnp.int32(0)
    for o in range(op_count):
        first[o] = total * 2
        total = total + lax.div(count[o] + 1, 2)

    def clear(i, c):
        lists[0, i] = 0
        lists[1, i] = 0
        lists[2, i] = 0
        return c

    lax.fori_loop(0, slots, clear, 0)

    def place(k, c):
        o = op_ref[k]
        spot = first[o]
        first[o] = spot + 1
        lists[0, spot] = k
        lists[1, spot] = 1
        lists[2, lax.div(spot, 2)] = o
        return c

    lax.fori_loop(0, terms, place, 0)

    sums[...] = jnp.zeros_like(sums)

    def pairs(i, c):
        lefts, rights, ops_at = [], [], []
        for at in (2 * i, 2 * i + 1):
            k1, k2 = lists[0, 2 * at], lists[0, 2 * at + 1]
            lefts += [left_ref[0, k1], left_ref[0, k2]]
            r1, r2 = right_ref[0, k1], right_ref[0, k2]
            r1 = jnp.where(lists[1, 2 * at] > 0, r1, jnp.zeros_like(r1))
            r2 = jnp.where(lists[1, 2 * at + 1] > 0, r2, jnp.zeros_like(r2))
            rights.append(jnp.concatenate([r1, r2], axis=0))
            ops_at.append(lists[2, at])
        v = jnp.dot(
            jnp.concatenate(lefts, axis=0), x_ref[0], preferred_element_type=jnp.float32
        ).astype(jnp.bfloat16)
        for j in range(2):
            w = v[2 * j * blk : 2 * (j + 1) * blk]
            both = [
                jnp.concatenate(
                    [w[:blk, p * blk : (p + 1) * blk], w[blk:, p * blk : (p + 1) * blk]], axis=1
                )
                for p in range(size_p)
            ]
            m = jnp.dot(
                jnp.concatenate(both, axis=0), rights[j], preferred_element_type=jnp.float32
            )
            for p in range(size_p):
                rows = pl.ds(p * pitch, blk)
                sums[ops_at[j], rows, :] = sums[ops_at[j], rows, :] + m[p * blk : (p + 1) * blk]
        return c

    lax.fori_loop(0, lax.div(total + 1, 2), pairs, 0)

    flat = sums.reshape(op_count * size_p * pitch, blk)
    opmat = opmat_ref[...]
    depth = op_count * size_p

    def mix(i, c):
        for u in range(4):
            a = i * 8 + u * 2
            y = jnp.concatenate(
                [flat[pl.ds(a, depth, stride=pitch), :], flat[pl.ds(a + 1, depth, stride=pitch), :]],
                axis=1,
            )
            high = y.astype(jnp.bfloat16)
            low = (y - high.astype(jnp.float32)).astype(jnp.bfloat16)
            m = jnp.dot(
                opmat,
                jnp.concatenate([high, low], axis=0),
                preferred_element_type=jnp.float32,
            )
            base = pl.multiple_of(i * 8 * size_p, size_p) + u * 2 * size_p
            base = pl.multiple_of(base, size_p)
            out_ref[0, pl.ds(base, size_p), :] = m[:, :blk]
            out_ref[0, pl.ds(pl.multiple_of(base + size_p, size_p), size_p), :] = m[:, blk:]
        return c

    lax.fori_loop(0, blk // 8, mix, 0)


def local_terms(x, left, right, term_op, ops):
    sectors, terms, blk, _ = left.shape
    op_count, size_p, _ = ops.shape
    width = x.shape[2]
    opmat = jnp.transpose(ops, (1, 0, 2)).reshape(size_p, op_count * size_p)
    opmat = jnp.concatenate([opmat, opmat], axis=1)
    flops = 4 * sectors * terms * blk * blk * width
    return pl.pallas_call(
        functools.partial(terms_kernel, size_p),
        out_shape=jax.ShapeDtypeStruct((sectors, blk * size_p, blk), jnp.float32),
        grid=(sectors,),
        in_specs=[
            pl.BlockSpec(memory_space=pltpu.SMEM),
            pl.BlockSpec(opmat.shape, lambda s: (0, 0)),
            pl.BlockSpec((1, blk, width), lambda s: (s, 0, 0)),
            pl.BlockSpec((1, terms, blk, blk), lambda s: (s, 0, 0, 0)),
            pl.BlockSpec((1, terms, blk, blk), lambda s: (s, 0, 0, 0)),
        ],
        out_specs=pl.BlockSpec((1, blk * size_p, blk), lambda s: (s, 0, 0)),
        scratch_shapes=[
            pltpu.VMEM((op_count, size_p * (blk + 8), blk), jnp.float32),
            pltpu.SMEM((op_count,), jnp.int32),
            pltpu.SMEM((op_count,), jnp.int32),
            pltpu.SMEM((3, terms + op_count + 8), jnp.int32),
        ],
        compiler_params=pltpu.CompilerParams(vmem_limit_bytes=44 * 2**20),
        cost_estimate=pl.CostEstimate(
            flops=flops, bytes_accessed=4 * sectors * terms * blk * blk, transcendentals=0
        ),
        name="terms",
    )(term_op, opmat, x, left, right)


def merge(stats, nb):
    xx, xh = stats[:, 0:1], stats[:, 1:2]
    rr, xr = stats[:, 2 + nb : 3 + nb], stats[:, 3 + nb : 4 + nb]
    q = xh / (xx + 1e-6)
    total = jnp.sum(stats, axis=0)
    all_q = total[1:2] / (total[0:1] + 1e-6)
    gap = q - all_q[None]
    rr = jnp.sum(rr + 2.0 * gap * xr + gap * gap * xx, axis=0)
    xr = jnp.sum(xr + gap * xx, axis=0)
    return jnp.concatenate(
        [total[: 2 + nb], rr, xr, jnp.zeros((4 - nb, total.shape[1]), jnp.float32)], axis=0
    ), all_q


def finish_kernel(
    n,
    groups,
    cells,
    dims_ref,
    level_ref,
    part_ref,
    psi_ref,
    basis_hbm,
    hpsi_ref,
    corr_ref,
    stat_ref,
    basis_ref,
    mine,
    theirs,
    away,
    landed,
    slots_m,
    slots_s,
    tile,
    basis_sem,
    load_sem,
    send1,
    recv1,
    send2,
    recv2,
    send3,
    recv3,
):
    row = lax.axis_index("sector")
    me = lax.axis_index("mpo")
    chips = n // 2
    core, chip = lax.rem(me, 2), lax.div(me, 2)
    sib = chip * 2 + 1 - core
    sectors, rows, width = psi_ref.shape
    nb = basis_ref.shape[0]
    blk = part_ref.shape[2]
    size_p = width // blk
    chunk = rows * size_p

    barrier = pltpu.get_barrier_semaphore()
    for j in range(1, n):
        pl.semaphore_signal(
            barrier, inc=1, device_id=(row, lax.rem(me + j, n)), device_id_type=MESH
        )
    for j in range(1, groups):
        pl.semaphore_signal(
            barrier, inc=1, device_id=(lax.rem(row + j, groups), me), device_id_type=MESH
        )
    basis_copy = pltpu.make_async_copy(basis_hbm, basis_ref, basis_sem)
    pl.semaphore_wait(barrier, n + groups - 2)

    def part(hop, which, s):
        block = lax.rem(chip + hop, chips) * 2 + which
        return part_ref.at[s, pl.ds(pl.multiple_of(block * chunk, chunk), chunk)]

    order = list(range(1, chips)) + [0]
    loads, swaps, sends = {}, {}, {}
    for hop in order:
        for s in range(sectors):
            swaps[hop, s] = pltpu.make_async_remote_copy(
                src_ref=part(hop, 1 - core, s),
                dst_ref=theirs.at[hop, s],
                send_sem=send1.at[hop, s],
                recv_sem=recv1.at[hop, s],
                device_id=(row, sib),
                device_id_type=MESH,
            )
            swaps[hop, s].start()
            loads[hop, s] = pltpu.make_async_copy(
                part(hop, core, s), mine.at[hop, s], load_sem.at[hop, s]
            )
            loads[hop, s].start()
    basis_copy.start()
    for hop in order:
        for s in range(sectors):
            loads[hop, s].wait()
            swaps[hop, s].wait_recv()
            if hop == 0:
                mine[0, s] = mine[0, s] + theirs[0, s]
            else:
                away[hop - 1, s] = (mine[hop, s] + theirs[hop, s]).astype(jnp.bfloat16)
                sends[hop, s] = pltpu.make_async_remote_copy(
                    src_ref=away.at[hop - 1, s],
                    dst_ref=landed.at[hop - 1, s],
                    send_sem=send2.at[hop, s],
                    recv_sem=recv2.at[hop, s],
                    device_id=(row, lax.rem(chip + hop, chips) * 2 + core),
                    device_id_type=MESH,
                )
                sends[hop, s].start()
    basis_copy.wait()

    row_at = me * rows + lax.broadcasted_iota(jnp.int32, (rows, blk), 0)
    col_at = lax.broadcasted_iota(jnp.int32, (rows, blk), 1)
    zero = jnp.zeros((rows, blk), jnp.float32)
    xx, xh, bh = zero, zero, [zero] * nb
    for s in range(sectors):
        for hop in range(1, chips):
            sends[hop, s].wait_recv()
            mine[0, s] = mine[0, s] + landed[hop - 1, s].astype(jnp.float32)
        mask = (row_at < dims_ref[s, 0]) & (col_at < dims_ref[s, 1])
        level = level_ref[s]
        for p in range(size_p):
            cols = slice(p * blk, (p + 1) * blk)
            spots = pl.ds(p, rows, stride=size_p)
            core_p = mine[0, s, spots, :]
            x = jnp.where(mask, psi_ref[s, :, cols].astype(jnp.float32), zero)
            h = jnp.where(mask, level * x + core_p, zero)
            hpsi_ref[s, :, cols] = h
            corr_ref[s, :, cols] = x
            xx = xx + x * x
            xh = xh + x * h
            bh = [bh[j] + basis_ref[j, s, :, cols] * h for j in range(nb)]

    def whole(v):
        v = jnp.sum(jnp.sum(v, axis=0, keepdims=True), axis=1, keepdims=True)
        return jnp.broadcast_to(v, (1, blk))

    xx, xh, bh = whole(xx), whole(xh), [whole(b) for b in bh]
    q = xh / (xx + 1e-6)
    rr, xr = zero, zero
    for s in range(sectors):
        for p in range(size_p):
            cols = slice(p * blk, (p + 1) * blk)
            x = corr_ref[s, :, cols]
            r = hpsi_ref[s, :, cols] - q * x
            rr = rr + r * r
            xr = xr + x * r
    stats = jnp.concatenate(
        [xx, xh] + bh + [whole(rr), whole(xr), jnp.zeros((4 - nb, blk), jnp.float32)], axis=0
    )

    def spread(level_no, stats, slots, count, mine_at, target):
        tile[level_no] = stats
        slots[mine_at] = stats
        for j in range(1, count):
            pltpu.make_async_remote_copy(
                src_ref=tile.at[level_no],
                dst_ref=slots.at[mine_at],
                send_sem=send3.at[level_no],
                recv_sem=recv3.at[level_no],
                device_id=target(j),
                device_id_type=MESH,
            ).start()
        some = slots.at[pl.ds(0, count - 1)]
        pltpu.make_async_copy(some, some, recv3.at[level_no]).wait()
        pltpu.make_async_copy(some, some, send3.at[level_no]).wait()
        return merge(slots[...], nb)

    stats, q = spread(0, stats, slots_m, n, me, lambda j: (row, lax.rem(me + j, n)))
    stats, q = spread(1, stats, slots_s, groups, row, lambda j: (lax.rem(row + j, groups), me))
    stat_ref[...] = jnp.concatenate([q, stats[1:]], axis=0)
    scale = 1.0 / jnp.sqrt(stats[2 + nb : 3 + nb] / cells + 1e-6)
    for s in range(sectors):
        for p in range(size_p):
            cols = slice(p * blk, (p + 1) * blk)
            corr_ref[s, :, cols] = (hpsi_ref[s, :, cols] - q * corr_ref[s, :, cols]) * scale
    for s in range(sectors):
        for hop in order:
            swaps[hop, s].wait_send()
            if hop:
                sends[hop, s].wait_send()


def finish(parts, psi, basis, dims, level, n, groups):
    sectors, rows, width = psi.shape
    nb = basis.shape[0]
    blk = parts.shape[2]
    chips = n // 2
    chunk = rows * (width // blk)
    cells = float(sectors * groups * rows * n * width)
    smem = pl.BlockSpec(memory_space=pltpu.SMEM)
    vmem = pl.BlockSpec(memory_space=pltpu.VMEM)
    far = pl.BlockSpec(memory_space=pl.ANY)
    dma = pltpu.SemaphoreType.DMA
    like = jax.ShapeDtypeStruct(psi.shape, jnp.float32)
    return pl.pallas_call(
        functools.partial(finish_kernel, n, groups, cells),
        out_shape=(like, like, jax.ShapeDtypeStruct((8, blk), jnp.float32)),
        in_specs=[smem, smem, far, vmem, far],
        out_specs=(vmem, vmem, vmem),
        scratch_shapes=[
            pltpu.VMEM(basis.shape, jnp.float32),
            pltpu.VMEM((chips, sectors, chunk, blk), jnp.float32),
            pltpu.VMEM((chips, sectors, chunk, blk), jnp.float32),
            pltpu.VMEM((max(chips - 1, 1), sectors, chunk, blk), jnp.bfloat16),
            pltpu.VMEM((max(chips - 1, 1), sectors, chunk, blk), jnp.bfloat16),
            pltpu.VMEM((n, 8, blk), jnp.float32),
            pltpu.VMEM((groups, 8, blk), jnp.float32),
            pltpu.VMEM((2, 8, blk), jnp.float32),
            dma(()),
            dma((chips, sectors)),
            dma((chips, sectors)),
            dma((chips, sectors)),
            dma((chips, sectors)),
            dma((chips, sectors)),
            dma((2,)),
            dma((2,)),
        ],
        compiler_params=pltpu.CompilerParams(
            collective_id=1, has_side_effects=True, vmem_limit_bytes=32 * 2**20
        ),
        name="finish",
    )(dims, level, parts, psi, basis)


def body(n, groups, psi, left_env, right_env, term_op, ops, energy, charge, block_dims, basis):
    blk = left_env.shape[-1]
    sectors, rows, width = psi.shape
    x = gather(psi, n)
    rows_ok = jnp.arange(blk, dtype=jnp.int32)[None, :, None] < block_dims[:, 0][:, None, None]
    cols_ok = (jnp.arange(width, dtype=jnp.int32) % blk)[None, None, :] < block_dims[:, 1][
        :, None, None
    ]
    x = jnp.where(rows_ok & cols_ok, x, jnp.zeros_like(x))
    parts = local_terms(x, left_env, right_env, term_op, ops)
    hot = (charge[:, None] == jnp.arange(energy.shape[0], dtype=jnp.int32)[None, :]).astype(
        jnp.float32
    )
    level = jnp.sum(hot * energy[None, :], axis=1)
    hpsi, correction, stats = finish(parts, psi, basis, block_dims, level, n, groups)
    return (hpsi, correction, stats[0, 0], stats[2 : 2 + basis.shape[0], 0])


def solution(mesh):
    placed = (
        P("sector", "mpo", None),
        P("sector", "mpo", None, None),
        P("sector", "mpo", None, None),
        P("mpo"),
        P(),
        P(),
        P("sector"),
        P("sector", None),
        P(None, "sector", "mpo", None),
    )
    return jax.shard_map(
        functools.partial(body, mesh.shape["mpo"], mesh.shape["sector"]),
        mesh=mesh,
        in_specs=placed,
        out_specs=(P("sector", "mpo", None), P("sector", "mpo", None), P(), P()),
        check_vma=False,
    )
```

profile of v0, /device:TPU:0, one launch (start us, length us, event | category | flops | bytes accessed | tf_op | source)
XLA Modules:
  0.0 75.9 jit_solution(225110678184710212)
XLA Ops:
  0.6 0.0 copy-start.6
  0.6 0.0 copy-start.3
  0.7 0.0 copy-start.5
  0.7 1.1 %slice_reduce_fusion.2 = (s32[2]{0:T(128)S(1)}, s32[2]{0:T(128)S(1)}) fusion(s32[2,2]{1,0:T(2,128)} %dims_ref.1), kind=kLoop, calls=%fused_computation.12 | loop fusion | bytes 32 | tf_op jit(solution)/shard_map/slice | solution.py:457
  1.7 0.1 broadcast_compare_fusion
  1.8 0.1 iota_compare_fusion
  1.9 12.1 %gather.1 = bf16[2,128,2048]{2,1,0:T(8,128)(2,1)} custom-call(bf16[2,32,2048]{2,1,0:T(8,128)(2,1)} %psi_ref.3), custom_call_target="tpu_custom_call" | custom-call | tf_op jit(solution)/shard_map/gather/pallas_call | solution.py:82
  14.0 1.6 %and_select_fusion.x_ref = bf16[2,128,2048]{2,1,0:T(8,128)(2,1)S(1)} fusion(bf16[2,128,2048]{2,1,0:T(8,128)(2,1)} %gather.1, pred[2,2048]{1,0:T(4,128)(4,1)S(1)} %broadcast_compare_fusion, pred[2,128]{1,0:T(4,128)(4,1)S(1)} %iota_compare_fusion), kind=kLoop, calls=%fused_computation | loop fusion | flops 1048576 | bytes 2101504 | tf_op jit(solution)/shard_map/jit(_where)/select_n | solution.py:461
  15.6 0.0 copy-done.6
  15.7 0.1 reshape.80
  15.8 0.0 copy-done.3
  15.8 0.0 copy-done.5
  15.8 0.0 copy-start.4
  15.8 1.6 %copy-done.4 = bf16[2,32,128,128]{3,2,1,0:T(8,128)(2,1)S(1)} copy-done((bf16[2,32,128,128]{3,2,1,0:T(8,128)(2,1)S(1)}, bf16[2,32,128,128]{3,2,1,0:T(8,128)(2,1)}, u32[]{:S(2)}) %copy-start.4) | copy-done | bytes 2097176
  17.4 0.0 copy-start.7
  17.4 0.0 copy-start.8
  17.4 0.0 copy-start
  17.4 0.0 copy-start.1
  17.4 0.0 copy-start.2
  17.4 35.7 %terms.1.part_ref = f32[2,2048,128]{2,1,0:T(8,128)S(1)} custom-call(s32[32]{0:T(128)S(1)} %copy-done.5, bf16[16,256]{1,0:T(8,128)(2,1)S(1)} %pad_maximum_fusion.opmat_ref, bf16[2,128,2048]{2,1,0:T(8,128)(2,1)S(1)} %and_select_fusion.x_ref, bf16[2,32,128,128]{3,2,1,0:T(8,128)(2,1)S(1)} %copy-done.3, bf16[2,32,128,128]{3,2,1,0:T(8,128)(2,1)S(1)} %copy-done.4), custom_call_target="tpu_custom_call" | custom-call | flops 8589934592 | bytes 4194304 | tf_op jit(solution)/shard_map/terms/pallas_call | solution.py:206
  53.1 0.0 copy-done.7
  53.1 0.0 copy-done.8
  53.1 0.2 fusion.3.level_ref
  53.3 0.0 copy-done
  53.3 0.0 copy-done.1
  53.3 0.0 copy-done.2
  53.3 19.9 %finish.1 = (f32[2,32,2048]{2,1,0:T(8,128)S(1)}, f32[2,32,2048]{2,1,0:T(8,128)S(1)}, f32[8,128]{1,0:T(8,128)S(1)}) custom-call(s32[2,2]{1,0:T(2,128)S(1)} %copy-done.2, f32[2]{0:T(128)S(1)} %fusion.3.level_ref, f32[2,2048,128]{2,1,0:T(8,128)S(1)} %terms.1.part_ref, bf16[2,32,2048]{2,1,0:T(8,128)(2,1)S(1)} %copy-done.1, f32[3,2,32,2048]{3,2,1,0:T(8,128)S(1)} %copy-done), custom_call_target="tpu_custom_call" | custom-call | tf_op jit(solution)/shard_map/finish/pallas_call | solution.py:423
  73.2 0.5 slice.17
  73.7 0.6 slice_reduce_fusion
  74.3 0.8 %copy.18 = f32[2,32,2048]{2,1,0:T(8,128)} copy(f32[2,32,2048]{2,1,0:T(8,128)S(1)} %get-tuple-element.16) | data formatting | bytes 1048576
  75.1 0.8 %copy.19 = f32[2,32,2048]{2,1,0:T(8,128)} copy(f32[2,32,2048]{2,1,0:T(8,128)S(1)} %get-tuple-element.17) | data formatting | bytes 1048576
  (3 shorter events, 0.0 us)
Async XLA Ops:
  0.6 15.0 %copy-start.6 = (bf16[8,16,16]{2,1,0:T(8,128)(2,1)S(1)}, bf16[8,16,16]{2,1,0:T(8,128)(2,1)}, u32[]{:S(2)}) copy-start(bf16[8,16,16]{2,1,0:T(8,128)(2,1)} %param.13) | copy-start | bytes 12292
  0.6 15.1 %copy-start.3 = (bf16[2,32,128,128]{3,2,1,0:T(8,128)(2,1)S(1)}, bf16[2,32,128,128]{3,2,1,0:T(8,128)(2,1)}, u32[]{:S(2)}) copy-start(bf16[2,32,128,128]{3,2,1,0:T(8,128)(2,1)} %left_ref.1) | copy-start | bytes 6291460
  0.7 15.1 %copy-start.5 = (s32[32]{0:T(128)S(1)}, s32[32]{0:T(128)}, u32[]{:S(2)}) copy-start(s32[32]{0:T(128)} %op_ref.1) | copy-start | bytes 388
  15.8 1.6 %copy-start.4 = (bf16[2,32,128,128]{3,2,1,0:T(8,128)(2,1)S(1)}, bf16[2,32,128,128]{3,2,1,0:T(8,128)(2,1)}, u32[]{:S(2)}) copy-start(bf16[2,32,128,128]{3,2,1,0:T(8,128)(2,1)} %right_ref.1) | copy-start | bytes 6291460
  17.4 35.7 %copy-start.7 = (f32[16]{0:T(128)S(1)}, f32[16]{0:T(128)}, u32[]{:S(2)}) copy-start(f32[16]{0:T(128)} %param.14) | copy-start | bytes 196
  17.4 35.7 %copy-start.8 = (s32[2]{0:T(128)S(1)}, s32[2]{0:T(128)}, u32[]{:S(2)}) copy-start(s32[2]{0:T(128)} %param.15) | copy-start | bytes 28
  17.4 35.9 %copy-start = (f32[3,2,32,2048]{3,2,1,0:T(8,128)S(1)}, f32[3,2,32,2048]{3,2,1,0:T(8,128)}, u32[]{:S(2)}) copy-start(f32[3,2,32,2048]{3,2,1,0:T(8,128)} %basis_hbm.1) | copy-start | bytes 4718596
  17.4 35.9 %copy-start.1 = (bf16[2,32,2048]{2,1,0:T(8,128)(2,1)S(1)}, bf16[2,32,2048]{2,1,0:T(8,128)(2,1)}, u32[]{:S(2)}) copy-start(bf16[2,32,2048]{2,1,0:T(8,128)(2,1)} %psi_ref.3) | copy-start | bytes 786436
  17.4 35.9 %copy-start.2 = (s32[2,2]{1,0:T(2,128)S(1)}, s32[2,2]{1,0:T(2,128)}, u32[]{:S(2)}) copy-start(s32[2,2]{1,0:T(2,128)} %dims_ref.1) | copy-start | bytes 52
where the time goes:
time: 77.5 us; the launch traced here: 75.9 us
  Pallas kernels  70.4 us (91%)
  local copies, waits for them, and re-layouts  5.5 us (7%)
  other arithmetic  1.94 us (3%)
    pallas_call x1, Pallas kernels, local_terms(): pl.pallas_call(functools.partial(terms_kernel, size_p), out_shape=jax.Sha...  35.7 us
    pallas_call x1, Pallas kernels, finish(): pl.pallas_call(functools.partial(finish_kernel, n, groups, cells), out_sh...  22.6 us
    pallas_call x1, Pallas kernels, gather(): pl.pallas_call(functools.partial(gather_kernel, n, sectors, flat), out_sh...  12.1 us
    unnamed x20, local copies, waits for them, and re-layouts  3.21 us
    select_n x1, other arithmetic, body(): x = jnp.where(rows_ok & cols_ok, x, jnp.zeros_like(x))  1.6 us

commit v1 on v0

v1 whole, which is shorter than its diff:
```python
import functools

import jax
import jax.numpy as jnp
from jax import lax
from jax.experimental import pallas as pl
from jax.experimental.pallas import tpu as pltpu
from jax.sharding import PartitionSpec as P

MESH = pl.DeviceIdType.MESH
F32, BF16, I32 = jnp.float32, jnp.bfloat16, jnp.int32
SUB = 8
CHUNKS = 2
PARTS = 4


def term_table(op_ref, terms, pairs):
    lane = lax.broadcasted_iota(I32, (terms, 128), 1)
    sub = lax.broadcasted_iota(I32, (terms, 128), 0)
    lane1 = lax.broadcasted_iota(I32, (1, 128), 1)
    col = jnp.zeros((terms, 128), I32)
    row = jnp.full((1, 128), -1, I32)
    for k in range(terms):
        o = op_ref[k]
        col = jnp.where(sub == k, o, col)
        row = jnp.where(lane1 == k, o, row)
    row = jnp.broadcast_to(row, (terms, 128))
    one, zero = jnp.ones((terms, 128), I32), jnp.zeros((terms, 128), I32)

    def along(mask, axis):
        return jnp.sum(jnp.where(mask, one, zero), axis=axis, keepdims=True)

    same = col == row
    rank_col = jnp.broadcast_to(along(same & (lane < sub), 1), (terms, 128))
    rank_row = jnp.broadcast_to(along(same & (sub < lane), 0), (terms, 128))
    heads = (row >= 0) & ((rank_row & 1) == 0)
    base = jnp.broadcast_to(along((row < col) & heads, 1), (terms, 128))
    place = 2 * base + rank_col
    hit = place == lane
    index = jnp.sum(jnp.where(hit, sub, zero), axis=0, keepdims=True)
    valid = along(hit, 0) > 0
    start = along(hit & (rank_col == 0), 0) > 0
    even = (rank_col & 1) == 0
    own = along(even & (col == lane), 0)
    upto = along(even & (col <= lane), 0)
    right = jnp.where(valid, index, terms)
    prev = jnp.where(valid & jnp.logical_not(start), (lane1 >> 1) - 1, pairs)
    last = jnp.where(own > 0, upto - 1, pairs)
    return jnp.concatenate([index, right, prev, last, jnp.zeros((4, 128), I32)], axis=0)


def mixing(ops_ref, om_ref):
    op_count, size_p, _ = ops_ref.shape
    wide = size_p * SUB
    up = (
        lax.broadcasted_iota(I32, (wide, size_p), 0) // SUB
        == lax.broadcasted_iota(I32, (wide, size_p), 1)
    ).astype(F32).astype(BF16)
    across = (
        lax.broadcasted_iota(I32, (size_p, wide), 1) // SUB
        == lax.broadcasted_iota(I32, (size_p, wide), 0)
    ).astype(F32).astype(BF16)
    diagonal = (lax.broadcasted_iota(I32, (wide, wide), 0) % SUB) == (
        lax.broadcasted_iota(I32, (wide, wide), 1) % SUB
    )
    for o in range(op_count):
        t = jnp.dot(up, ops_ref[o], preferred_element_type=F32).astype(BF16)
        u = jnp.dot(t, across, preferred_element_type=F32)
        u = jnp.where(diagonal, u, jnp.zeros_like(u)).astype(BF16)
        om_ref[:, o * wide : (o + 1) * wide] = u
        om_ref[:, (op_count + o) * wide : (op_count + o + 1) * wide] = u


def merge(stats, nb):
    xx, xh = stats[:, 0:1], stats[:, 1:2]
    rr, xr = stats[:, 2 + nb : 3 + nb], stats[:, 3 + nb : 4 + nb]
    q = xh / (xx + 1e-6)
    total = jnp.sum(stats, axis=0)
    all_q = total[1:2] / (total[0:1] + 1e-6)
    gap = q - all_q[None]
    rr = jnp.sum(rr + 2.0 * gap * xr + gap * gap * xx, axis=0)
    xr = jnp.sum(xr + gap * xx, axis=0)
    return jnp.concatenate(
        [total[: 2 + nb], rr, xr, jnp.zeros((4 - nb, total.shape[1]), F32)], axis=0
    ), all_q


def kernel(
    n,
    groups,
    cells,
    pairs,
    dims_ref,
    charge_ref,
    energy_ref,
    op_ref,
    ops_ref,
    psi_hbm,
    left_hbm,
    right_hbm,
    basis_hbm,
    hpsi_ref,
    corr_ref,
    stat_ref,
    xraw,
    xt,
    lraw,
    rraw,
    lt,
    rt,
    v_ref,
    sums,
    om_ref,
    turned,
    part_ref,
    theirs,
    away,
    landed,
    basis_ref,
    tab_v,
    tab,
    slots_m,
    slots_s,
    tile,
    own_sem,
    env_sem,
    basis_sem,
    tab_sem,
    gsend,
    grecv,
    fsend,
    frecv,
    send1,
    recv1,
    send2,
    recv2,
    send3,
    recv3,
):
    row = lax.axis_index("sector")
    me = lax.axis_index("mpo")
    chips = n // 2
    core, chip = lax.rem(me, 2), lax.div(me, 2)
    sib = chip * 2 + 1 - core
    sectors, terms, blk, _ = lraw.shape
    rows, cw = xraw.shape[3:]
    size_p = part_ref.shape[1]
    op_count = ops_ref.shape[0]
    nb = basis_ref.shape[0]
    qn = cw // blk
    pn = size_p // PARTS
    width = size_p * blk

    def at(hop):
        return lax.rem(chip + hop, chips) * 2

    envs = {}
    for s in range(sectors):
        envs[0, s] = pltpu.make_async_copy(left_hbm.at[s], lraw.at[s], env_sem.at[0, s])
        envs[1, s] = pltpu.make_async_copy(right_hbm.at[s], rraw.at[s], env_sem.at[1, s])
    own = {}
    for s in range(sectors):
        for c in range(CHUNKS):
            own[s, c] = pltpu.make_async_copy(
                psi_hbm.at[s, :, pl.ds(c * cw, cw)], xraw.at[s, c, me], own_sem.at[s, c]
            )
    barrier = pltpu.get_barrier_semaphore()
    for j in range(1, n):
        pl.semaphore_signal(
            barrier, inc=1, device_id=(row, lax.rem(me + j, n)), device_id_type=MESH
        )
    for j in range(1, groups):
        pl.semaphore_signal(
            barrier, inc=1, device_id=(lax.rem(row + j, groups), me), device_id_type=MESH
        )
    envs[0, 0].start()
    for copy in own.values():
        copy.start()
    envs[1, 0].start()
    for s in range(1, sectors):
        envs[0, s].start()
        envs[1, s].start()
    tab_v[...] = term_table(op_ref, terms, pairs)
    table = pltpu.make_async_copy(tab_v, tab, tab_sem)
    table.start()
    pl.semaphore_wait(barrier, n + groups - 2)

    def push(src, block, s, c, to, ssem, rsem):
        return pltpu.make_async_remote_copy(
            src_ref=src,
            dst_ref=xraw.at[s, c, block],
            send_sem=ssem,
            recv_sem=rsem,
            device_id=(row, to),
            device_id_type=MESH,
        )

    far, near, relay = {}, {}, {}
    for s in range(sectors):
        for c in range(CHUNKS):
            i = s * CHUNKS + c
            src = psi_hbm.at[s, :, pl.ds(c * cw, cw)]
            for hop in range(1, chips):
                far[hop, s, c] = push(
                    src, me, s, c, at(hop) + core, gsend.at[hop, i], grecv.at[hop, i]
                )
                far[hop, s, c].start()
            near[s, c] = push(src, me, s, c, sib, gsend.at[0, i], grecv.at[0, i])
            near[s, c].start()

    def pass_on(s, c):
        i = s * CHUNKS + c
        for hop in range(1, chips):
            far[hop, s, c].wait_recv()
            block = at(chips - hop) + core
            relay[hop, s, c] = push(
                xraw.at[s, c, block], block, s, c, sib, fsend.at[hop, i], frecv.at[hop, i]
            )
            relay[hop, s, c].start()

    def arrived(s, c):
        own[s, c].wait()
        near[s, c].wait_recv()
        for hop in range(1, chips):
            relay[hop, s, c].wait_recv()

    basis_copy = pltpu.make_async_copy(basis_hbm, basis_ref, basis_sem)
    basis_copy.start()
    sums[pairs] = jnp.zeros(sums.shape[1:], F32)

    def turn_left(s):
        envs[0, s].wait()

        def step(i, c):
            for u in range(4):
                k = i * 4 + u
                lt[s, :, pl.ds(pl.multiple_of(k * blk, blk), blk)] = lraw[s, k].T
            return c

        lax.fori_loop(0, terms // 4, step, 0)

    def turn_right(s):
        envs[1, s].wait()

        def step(i, c):
            for u in range(4):
                rt[s, i * 4 + u] = rraw[s, i * 4 + u].T
            return c

        lax.fori_loop(0, terms // 4, step, 0)
        rt[s, terms] = jnp.zeros((blk, blk), BF16)

    turn_left(0)
    pass_on(0, 0)
    mixing(ops_ref, om_ref)
    turn_right(0)
    for c in range(1, CHUNKS):
        pass_on(0, c)
    for s in range(1, sectors):
        turn_left(s)
        turn_right(s)
    table.wait()

    row_at = lax.broadcasted_iota(I32, (blk, blk), 0)
    col_at = lax.broadcasted_iota(I32, (blk, blk), 1)

    def assemble(s, c):
        arrived(s, c)
        ok = (row_at < dims_ref[s, 0]) & (col_at < dims_ref[s, 1])
        for q in range(qn):
            x = jnp.concatenate(
                [xraw[s, c, b, :, q * blk : (q + 1) * blk].astype(F32) for b in range(n)], axis=0
            )
            x = jnp.where(ok, x, jnp.zeros_like(x)).astype(BF16)
            xt[(c * qn + q) * blk : (c * qn + q + 1) * blk, :] = x.T

    def first(s, c):
        def step(i, carry):
            m = jnp.dot(
                xt[c * cw : (c + 1) * cw, :],
                lt[s, :, pl.ds(pl.multiple_of(i * 8 * blk, 8 * blk), 8 * blk)],
                preferred_element_type=F32,
            ).astype(BF16)
            for u in range(8):
                for q in range(qn):
                    v_ref[i * 8 + u, :, (c * qn + q) * blk : (c * qn + q + 1) * blk] = m[
                        q * blk : (q + 1) * blk, u * blk : (u + 1) * blk
                    ]
            return carry

        lax.fori_loop(0, terms // 8, step, 0)

    def second(s):
        def step(i, carry):
            for u in range(4):
                j = i * 4 + u
                r = jnp.concatenate([rt[s, tab[1, 2 * j]], rt[s, tab[1, 2 * j + 1]]], axis=1)
                v = jnp.concatenate([v_ref[tab[0, 2 * j]], v_ref[tab[0, 2 * j + 1]]], axis=0)
                m = jnp.dot(r, v, preferred_element_type=F32)
                prev = tab[2, 2 * j]
                for q in range(size_p):
                    sums[j, q] = sums[prev, q] + m[:, q * blk : (q + 1) * blk]
            return carry

        lax.fori_loop(0, pairs // 4, step, 0)

    def mix():
        wide = size_p * SUB

        def step(i, carry):
            both = []
            for t in range(4):
                b0 = pl.multiple_of((i * 4 + t) * SUB, SUB)
                high, low = [], []
                for o in range(op_count):
                    y = sums[tab[3, o], :, pl.ds(b0, SUB), :].reshape(wide, blk)
                    h = y.astype(BF16)
                    high.append(h)
                    low.append((y - h.astype(F32)).astype(BF16))
                both.append(jnp.concatenate(high + low, axis=0))
            m = jnp.dot(om_ref[...], jnp.concatenate(both, axis=1), preferred_element_type=F32)
            for t in range(4):
                b0 = pl.multiple_of((i * 4 + t) * SUB, SUB)
                turned[:, pl.ds(b0, SUB), :] = m[:, t * blk : (t + 1) * blk].reshape(
                    size_p, SUB, blk
                )
            return carry

        lax.fori_loop(0, blk // (4 * SUB), step, 0)

    order = list(range(1, chips)) + [0]
    swaps, sends = {}, {}

    def rows_of(block):
        return pl.ds(pl.multiple_of(block * rows, rows), rows)

    def turn_out(s):
        for g in range(PARTS):
            for p in range(g * pn, (g + 1) * pn):
                part_ref[s, p] = turned[p].T
            for hop in order:
                swaps[hop, s, g] = pltpu.make_async_remote_copy(
                    src_ref=part_ref.at[s, pl.ds(g * pn, pn), rows_of(at(hop) + 1 - core)],
                    dst_ref=theirs.at[hop, s, g],
                    send_sem=send1.at[hop, s * PARTS + g],
                    recv_sem=recv1.at[hop, s * PARTS + g],
                    device_id=(row, sib),
                    device_id_type=MESH,
                )
                swaps[hop, s, g].start()

    def send_far(s):
        for g in range(PARTS):
            for hop in range(1, chips):
                swaps[hop, s, g].wait_recv()
                y = part_ref[s, g * pn : (g + 1) * pn, rows_of(at(hop) + core), :] + theirs[hop, s, g]
                away[hop - 1, s, g] = y.reshape(pn * rows, blk).astype(BF16)
                sends[hop, s, g] = pltpu.make_async_remote_copy(
                    src_ref=away.at[hop - 1, s, g],
                    dst_ref=landed.at[hop - 1, s, g],
                    send_sem=send2.at[hop, s * PARTS + g],
                    recv_sem=recv2.at[hop, s * PARTS + g],
                    device_id=(row, at(hop) + core),
                    device_id_type=MESH,
                )
                sends[hop, s, g].start()

    zero = jnp.zeros((rows, blk), F32)
    mine_row = me * rows + lax.broadcasted_iota(I32, (rows, blk), 0)
    mine_col = lax.broadcasted_iota(I32, (rows, blk), 1)

    def finish(s, acc):
        xx, xh, bh = acc
        ok = (mine_row < dims_ref[s, 0]) & (mine_col < dims_ref[s, 1])
        level = energy_ref[charge_ref[s]]
        for g in range(PARTS):
            swaps[0, s, g].wait_recv()
            for hop in range(1, chips):
                sends[hop, s, g].wait_recv()
            for u in range(pn):
                p = g * pn + u
                c, q = p // qn, p % qn
                y = part_ref[s, p, rows_of(me), :] + theirs[0, s, g, u]
                for hop in range(1, chips):
                    y = y + landed[hop - 1, s, g, u * rows : (u + 1) * rows, :].astype(F32)
                x = xraw[s, c, me, :, q * blk : (q + 1) * blk].astype(F32)
                x = jnp.where(ok, x, zero)
                h = jnp.where(ok, level * x + y, zero)
                cols = slice(p * blk, (p + 1) * blk)
                hpsi_ref[s, :, cols] = h
                corr_ref[s, :, cols] = x
                xx = xx + x * x
                xh = xh + x * h
                bh = [bh[j] + basis_ref[j, s, :, cols] * h for j in range(nb)]
        return xx, xh, bh

    acc = (zero, zero, [zero] * nb)
    for s in range(sectors):
        for c in range(CHUNKS):
            assemble(s, c)
            first(s, c)
            if s + 1 < sectors:
                pass_on(s + 1, c)
        if s > 0:
            send_far(s - 1)
        second(s)
        mix()
        turn_out(s)
    basis_copy.wait()
    send_far(sectors - 1)
    for s in range(sectors):
        acc = finish(s, acc)
    xx, xh, bh = acc

    def whole(t):
        t = jnp.sum(jnp.sum(t, axis=0, keepdims=True), axis=1, keepdims=True)
        return jnp.broadcast_to(t, (1, blk))

    xx, xh, bh = whole(xx), whole(xh), [whole(b) for b in bh]
    q = xh / (xx + 1e-6)
    rr, xr = zero, zero
    for s in range(sectors):
        for p in range(size_p):
            cols = slice(p * blk, (p + 1) * blk)
            x = corr_ref[s, :, cols]
            r = hpsi_ref[s, :, cols] - q * x
            rr = rr + r * r
            xr = xr + x * r
    stats = jnp.concatenate(
        [xx, xh] + bh + [whole(rr), whole(xr), jnp.zeros((4 - nb, blk), F32)], axis=0
    )

    def spread(level_no, stats, slots, count, mine_at, target):
        tile[level_no] = stats
        slots[mine_at] = stats
        for j in range(1, count):
            pltpu.make_async_remote_copy(
                src_ref=tile.at[level_no],
                dst_ref=slots.at[mine_at],
                send_sem=send3.at[level_no],
                recv_sem=recv3.at[level_no],
                device_id=target(j),
                device_id_type=MESH,
            ).start()
        some = slots.at[pl.ds(0, count - 1)]
        pltpu.make_async_copy(some, some, recv3.at[level_no]).wait()
        pltpu.make_async_copy(some, some, send3.at[level_no]).wait()
        return merge(slots[...], nb)

    stats, q = spread(0, stats, slots_m, n, me, lambda j: (row, lax.rem(me + j, n)))
    stats, q = spread(1, stats, slots_s, groups, row, lambda j: (lax.rem(row + j, groups), me))
    stat_ref[...] = jnp.concatenate([q, stats[1:]], axis=0)
    scale = 1.0 / jnp.sqrt(stats[2 + nb : 3 + nb] / cells + 1e-6)
    for s in range(sectors):
        for p in range(size_p):
            cols = slice(p * blk, (p + 1) * blk)
            corr_ref[s, :, cols] = (hpsi_ref[s, :, cols] - q * corr_ref[s, :, cols]) * scale
    for copy in list(far.values()) + list(near.values()) + list(relay.values()):
        copy.wait_send()
    for copy in list(swaps.values()) + list(sends.values()):
        copy.wait_send()


def body(n, groups, psi, left_env, right_env, term_op, ops, energy, charge, block_dims, basis):
    sectors, rows, width = psi.shape
    _, terms, blk, _ = left_env.shape
    op_count, size_p, _ = ops.shape
    nb = basis.shape[0]
    chips = n // 2
    cells = float(sectors * groups * rows * n * width)
    pairs = -(-min(terms, (terms + op_count) // 2) // 4) * 4
    cw = width // CHUNKS
    pn = size_p // PARTS
    wide = size_p * SUB
    smem = pl.BlockSpec(memory_space=pltpu.SMEM)
    vmem = pl.BlockSpec(memory_space=pltpu.VMEM)
    far = pl.BlockSpec(memory_space=pl.ANY)
    dma = pltpu.SemaphoreType.DMA
    like = jax.ShapeDtypeStruct(psi.shape, F32)
    hops = max(chips - 1, 1)
    hpsi, correction, stats = pl.pallas_call(
        functools.partial(kernel, n, groups, cells, pairs),
        out_shape=(like, like, jax.ShapeDtypeStruct((8, blk), F32)),
        in_specs=[smem, smem, smem, smem, vmem, far, far, far, far],
        out_specs=(vmem, vmem, vmem),
        scratch_shapes=[
            pltpu.VMEM((sectors, CHUNKS, n, rows, cw), BF16),
            pltpu.VMEM((width, blk), BF16),
            pltpu.VMEM(left_env.shape, BF16),
            pltpu.VMEM(right_env.shape, BF16),
            pltpu.VMEM((sectors, blk, terms * blk), BF16),
            pltpu.VMEM((sectors, terms + 1, blk, blk), BF16),
            pltpu.VMEM((terms, blk, width), BF16),
            pltpu.VMEM((pairs + 1, size_p, blk, blk), F32),
            pltpu.VMEM((wide, 2 * op_count * wide), BF16),
            pltpu.VMEM((size_p, blk, blk), F32),
            pltpu.VMEM((sectors, size_p, blk, blk), F32),
            pltpu.VMEM((chips, sectors, PARTS, pn, rows, blk), F32),
            pltpu.VMEM((hops, sectors, PARTS, pn * rows, blk), BF16),
            pltpu.VMEM((hops, sectors, PARTS, pn * rows, blk), BF16),
            pltpu.VMEM(basis.shape, F32),
            pltpu.VMEM((8, 128), I32),
            pltpu.SMEM((8, 128), I32),
            pltpu.VMEM((n, 8, blk), F32),
            pltpu.VMEM((groups, 8, blk), F32),
            pltpu.VMEM((2, 8, blk), F32),
            dma((sectors, CHUNKS)),
            dma((2, sectors)),
            dma(()),
            dma(()),
            dma((chips, sectors * CHUNKS)),
            dma((chips, sectors * CHUNKS)),
            dma((chips, sectors * CHUNKS)),
            dma((chips, sectors * CHUNKS)),
            dma((chips, sectors * PARTS)),
            dma((chips, sectors * PARTS)),
            dma((chips, sectors * PARTS)),
            dma((chips, sectors * PARTS)),
            dma((2,)),
            dma((2,)),
        ],
        compiler_params=pltpu.CompilerParams(
            collective_id=0, has_side_effects=True, vmem_limit_bytes=61 * 2**20
        ),
        name="step",
    )(block_dims, charge, energy, term_op, ops, psi, left_env, right_env, basis)
    return (hpsi, correction, stats[0, 0], stats[2 : 2 + nb, 0])


def solution(mesh):
    placed = (
        P("sector", "mpo", None),
        P("sector", "mpo", None, None),
        P("sector", "mpo", None, None),
        P("mpo"),
        P(),
        P(),
        P("sector"),
        P("sector", None),
        P(None, "sector", "mpo", None),
    )
    return jax.shard_map(
        functools.partial(body, mesh.shape["mpo"], mesh.shape["sector"]),
        mesh=mesh,
        in_specs=placed,
        out_specs=(P("sector", "mpo", None), P("sector", "mpo", None), P(), P()),
        check_vma=False,
    )
```

time: 77.5 us -> 61.3 us (0.79); the launches traced: 75.9 us -> 60.9 us
  Pallas kernels: 70.4 us -> 54 us
  other arithmetic: 1.94 us -> 0 us
    pallas_call x3 -> x1, Pallas kernels: 70.4 us -> 54 us  [body(): pl.pallas_call(functools.partial(kernel, n, groups, cells, pairs), out_sh...]
    select_n x2 -> x0, other arithmetic: 1.6 us -> none  [the longest x1 1.6 us: body(): x = jnp.where(rows_ok & cols_ok, x, jnp.zeros_like(x))]
    unnamed x20 -> x2, local copies, waits for them, and re-layouts: 3.21 us -> 3.74 us
    slice x3 -> x2, local copies, waits for them, and re-layouts: 2.19 us -> 2.48 us  [body(): return (hpsi, correction, stats[0, 0], stats[2:2 + nb, 0])]
where the time goes in v1:
time: 61.3 us; the launch traced here: 60.9 us
  Pallas kernels  54 us (88%)
  local copies, waits for them, and re-layouts  6.23 us (10%)
  between operations  0.64 us (1%)
    pallas_call x1, Pallas kernels, body(): pl.pallas_call(functools.partial(kernel, n, groups, cells, pairs), out_sh...  54 us
    unnamed x2, local copies, waits for them, and re-layouts  3.74 us
    slice x2, local copies, waits for them, and re-layouts, body(): return (hpsi, correction, stats[0, 0], stats[2:2 + nb, 0])  2.48 us

profile of v1, /device:TPU:0, one launch (start us, length us, event | category | flops | bytes accessed | tf_op | source)
XLA Modules:
  0.0 60.9 jit_solution(14173585314289819317)
XLA Ops:
  0.6 54.0 %step.1 = (f32[2,32,2048]{2,1,0:T(8,128)}, f32[2,32,2048]{2,1,0:T(8,128)}, f32[8,128]{1,0:T(8,128)}) custom-call(s32[2,2]{1,0:T(2,128)} %dims_ref.1, s32[2]{0:T(128)} %charge_ref.1, f32[16]{0:T(128)} %energy_ref.1, s32[32]{0:T(128)} %op_ref.1, bf16[8,16,16]{2,1,0:T(8,128)(2,1)} %ops_ref.1, bf16[2,32,2048]{2,1,0:T(8,128)(2,1)} %psi_hbm.1, ...), custom_call_target="tpu_custom_call" | custom-call | tf_op jit(solution)/shard_map/step/pallas_call | solution.py:481
  54.7 1.2 %slice.6 = f32[1,1]{1,0:T(1,128)} slice(f32[8,128]{1,0:T(8,128)} %get-tuple-element.9), slice={[0:1], [0:1]} | slice | bytes 8 | tf_op jit(solution)/shard_map/slice | solution.py:527
  55.9 1.3 %slice_reduce_fusion = f32[3]{0:T(128)} fusion(f32[8,128]{1,0:T(8,128)} %get-tuple-element.9), kind=kLoop, calls=%fused_computation | loop fusion | bytes 24 | tf_op jit(solution)/shard_map/slice | solution.py:527
  57.2 1.9 %copy.15 = f32[2,32,2048]{2,1,0:T(8,128)} copy(f32[2,32,2048]{2,1,0:T(8,128)} %get-tuple-element.14) | data formatting | bytes 1048576
  59.0 1.9 %copy.16 = f32[2,32,2048]{2,1,0:T(8,128)} copy(f32[2,32,2048]{2,1,0:T(8,128)} %get-tuple-element.15) | data formatting | bytes 1048576

commit v2 on v1

--- a/solution.py
+++ b/solution.py
@@ -12,6 +12,7 @@
 SUB = 8
 CHUNKS = 2
 PARTS = 4
+FLAT = 64
 
 
 def term_table(op_ref, terms, pairs):
@@ -100,18 +101,15 @@
     right_hbm,
     basis_hbm,
     hpsi_ref,
-    corr_ref,
+    x_ref,
     stat_ref,
     xraw,
     xt,
-    lraw,
-    rraw,
     lt,
     rt,
     v_ref,
     sums,
     om_ref,
-    turned,
     part_ref,
     theirs,
     away,
@@ -139,10 +137,11 @@
 ):
     row = lax.axis_index("sector")
     me = lax.axis_index("mpo")
+    one_level = n * groups <= FLAT
     chips = n // 2
     core, chip = lax.rem(me, 2), lax.div(me, 2)
     sib = chip * 2 + 1 - core
-    sectors, terms, blk, _ = lraw.shape
+    sectors, terms, blk, _ = left_hbm.shape
     rows, cw = xraw.shape[3:]
     size_p = part_ref.shape[1]
     op_count = ops_ref.shape[0]
@@ -156,8 +155,10 @@
 
     envs = {}
     for s in range(sectors):
-        envs[0, s] = pltpu.make_async_copy(left_hbm.at[s], lraw.at[s], env_sem.at[0, s])
-        envs[1, s] = pltpu.make_async_copy(right_hbm.at[s], rraw.at[s], env_sem.at[1, s])
+        for i, src in enumerate((left_hbm, right_hbm)):
+            envs[i, s] = pltpu.make_async_copy(
+                src.at[s], v_ref.at[:, :, pl.ds((2 * s + i) * blk, blk)], env_sem.at[i, s]
+            )
     own = {}
     for s in range(sectors):
         for c in range(CHUNKS):
@@ -169,10 +170,14 @@
         pl.semaphore_signal(
             barrier, inc=1, device_id=(row, lax.rem(me + j, n)), device_id_type=MESH
         )
-    for j in range(1, groups):
-        pl.semaphore_signal(
-            barrier, inc=1, device_id=(lax.rem(row + j, groups), me), device_id_type=MESH
-        )
+    for i in range(1, groups):
+        for j in range(n if one_level else 1):
+            pl.semaphore_signal(
+                barrier,
+                inc=1,
+                device_id=(lax.rem(row + i, groups), lax.rem(me + j, n)),
+                device_id_type=MESH,
+            )
     envs[0, 0].start()
     for copy in own.values():
         copy.start()
@@ -183,7 +188,8 @@
     tab_v[...] = term_table(op_ref, terms, pairs)
     table = pltpu.make_async_copy(tab_v, tab, tab_sem)
     table.start()
-    pl.semaphore_wait(barrier, n + groups - 2)
+    mixing(ops_ref, om_ref)
+    pl.semaphore_wait(barrier, n * groups - 1 if one_level else n + groups - 2)
 
     def push(src, block, s, c, to, ssem, rsem):
         return pltpu.make_async_remote_copy(
@@ -234,7 +240,7 @@
         def step(i, c):
             for u in range(4):
                 k = i * 4 + u
-                lt[s, :, pl.ds(pl.multiple_of(k * blk, blk), blk)] = lraw[s, k].T
+                lt[s, :, pl.ds(pl.multiple_of(k * blk, blk), blk)] = v_ref[k, :, 2 * s * blk : (2 * s + 1) * blk].T
             return c
 
         lax.fori_loop(0, terms // 4, step, 0)
@@ -244,20 +250,19 @@
 
         def step(i, c):
             for u in range(4):
-                rt[s, i * 4 + u] = rraw[s, i * 4 + u].T
+                k = i * 4 + u
+                rt[s, k] = v_ref[k, :, (2 * s + 1) * blk : (2 * s + 2) * blk].T
             return c
 
         lax.fori_loop(0, terms // 4, step, 0)
         rt[s, terms] = jnp.zeros((blk, blk), BF16)
 
     turn_left(0)
-    pass_on(0, 0)
-    mixing(ops_ref, om_ref)
     turn_right(0)
-    for c in range(1, CHUNKS):
-        pass_on(0, c)
     for s in range(1, sectors):
         turn_left(s)
+    pass_on(0, 0)
+    for s in range(1, sectors):
         turn_right(s)
     table.wait()
 
@@ -274,21 +279,23 @@
             x = jnp.where(ok, x, jnp.zeros_like(x)).astype(BF16)
             xt[(c * qn + q) * blk : (c * qn + q + 1) * blk, :] = x.T
 
-    def first(s, c):
+    def first(begin, count, s):
+        some = next(k for k in (16, 8, 4, 2, 1) if terms % k == 0)
+
         def step(i, carry):
             m = jnp.dot(
-                xt[c * cw : (c + 1) * cw, :],
-                lt[s, :, pl.ds(pl.multiple_of(i * 8 * blk, 8 * blk), 8 * blk)],
+                xt[begin : begin + count, :],
+                lt[s, :, pl.ds(pl.multiple_of(i * some * blk, some * blk), some * blk)],
                 preferred_element_type=F32,
             ).astype(BF16)
-            for u in range(8):
-                for q in range(qn):
-                    v_ref[i * 8 + u, :, (c * qn + q) * blk : (c * qn + q + 1) * blk] = m[
+            for u in range(some):
+                for q in range(count // blk):
+                    v_ref[i * some + u, :, begin + q * blk : begin + (q + 1) * blk] = m[
                         q * blk : (q + 1) * blk, u * blk : (u + 1) * blk
                     ]
             return carry
 
-        lax.fori_loop(0, terms // 8, step, 0)
+        lax.fori_loop(0, terms // some, step, 0)
 
     def second(s):
         def step(i, carry):
@@ -304,7 +311,7 @@
 
         lax.fori_loop(0, pairs // 4, step, 0)
 
-    def mix():
+    def mix(s):
         wide = size_p * SUB
 
         def step(i, carry):
@@ -321,7 +328,7 @@
             m = jnp.dot(om_ref[...], jnp.concatenate(both, axis=1), preferred_element_type=F32)
             for t in range(4):
                 b0 = pl.multiple_of((i * 4 + t) * SUB, SUB)
-                turned[:, pl.ds(b0, SUB), :] = m[:, t * blk : (t + 1) * blk].reshape(
+                part_ref[s, :, pl.ds(b0, SUB), :] = m[:, t * blk : (t + 1) * blk].reshape(
                     size_p, SUB, blk
                 )
             return carry
@@ -337,7 +344,7 @@
     def turn_out(s):
         for g in range(PARTS):
             for p in range(g * pn, (g + 1) * pn):
-                part_ref[s, p] = turned[p].T
+                part_ref[s, p] = part_ref[s, p].T
             for hop in order:
                 swaps[hop, s, g] = pltpu.make_async_remote_copy(
                     src_ref=part_ref.at[s, pl.ds(g * pn, pn), rows_of(at(hop) + 1 - core)],
@@ -369,8 +376,12 @@
     mine_row = me * rows + lax.broadcasted_iota(I32, (rows, blk), 0)
     mine_col = lax.broadcasted_iota(I32, (rows, blk), 1)
 
-    def finish(s, acc):
-        xx, xh, bh = acc
+    def whole(t):
+        t = jnp.sum(jnp.sum(t, axis=0, keepdims=True), axis=1, keepdims=True)
+        return jnp.broadcast_to(t, (1, blk))
+
+    def finish(s):
+        xx, xh, bh = zero, zero, [zero] * nb
         ok = (mine_row < dims_ref[s, 0]) & (mine_col < dims_ref[s, 1])
         level = energy_ref[charge_ref[s]]
         for g in range(PARTS):
@@ -388,47 +399,42 @@
                 h = jnp.where(ok, level * x + y, zero)
                 cols = slice(p * blk, (p + 1) * blk)
                 hpsi_ref[s, :, cols] = h
-                corr_ref[s, :, cols] = x
+                x_ref[s, :, cols] = x
                 xx = xx + x * x
                 xh = xh + x * h
                 bh = [bh[j] + basis_ref[j, s, :, cols] * h for j in range(nb)]
-        return xx, xh, bh
-
-    acc = (zero, zero, [zero] * nb)
+        xx, xh, bh = whole(xx), whole(xh), [whole(b) for b in bh]
+        q = xh / (xx + 1e-6)
+        rr, xr = zero, zero
+        for p in range(size_p):
+            cols = slice(p * blk, (p + 1) * blk)
+            x = x_ref[s, :, cols]
+            r = hpsi_ref[s, :, cols] - q * x
+            rr = rr + r * r
+            xr = xr + x * r
+        return jnp.concatenate(
+            [xx, xh] + bh + [whole(rr), whole(xr), jnp.zeros((4 - nb, blk), F32)], axis=0
+        )
+
     for s in range(sectors):
         for c in range(CHUNKS):
             assemble(s, c)
-            first(s, c)
+            if s == 0:
+                for later in range(1, CHUNKS) if c == 0 else ():
+                    pass_on(0, later)
+                first(c * cw, cw, s)
             if s + 1 < sectors:
                 pass_on(s + 1, c)
         if s > 0:
+            first(0, width, s)
+        if s > 0:
             send_far(s - 1)
         second(s)
-        mix()
+        mix(s)
         turn_out(s)
     basis_copy.wait()
     send_far(sectors - 1)
-    for s in range(sectors):
-        acc = finish(s, acc)
-    xx, xh, bh = acc
-
-    def whole(t):
-        t = jnp.sum(jnp.sum(t, axis=0, keepdims=True), axis=1, keepdims=True)
-        return jnp.broadcast_to(t, (1, blk))
-
-    xx, xh, bh = whole(xx), whole(xh), [whole(b) for b in bh]
-    q = xh / (xx + 1e-6)
-    rr, xr = zero, zero
-    for s in range(sectors):
-        for p in range(size_p):
-            cols = slice(p * blk, (p + 1) * blk)
-            x = corr_ref[s, :, cols]
-            r = hpsi_ref[s, :, cols] - q * x
-            rr = rr + r * r
-            xr = xr + x * r
-    stats = jnp.concatenate(
-        [xx, xh] + bh + [whole(rr), whole(xr), jnp.zeros((4 - nb, blk), F32)], axis=0
-    )
+    stats, _ = merge(jnp.stack([finish(s) for s in range(sectors)]), nb)
 
     def spread(level_no, stats, slots, count, mine_at, target):
         tile[level_no] = stats
@@ -447,18 +453,72 @@
         pltpu.make_async_copy(some, some, send3.at[level_no]).wait()
         return merge(slots[...], nb)
 
-    stats, q = spread(0, stats, slots_m, n, me, lambda j: (row, lax.rem(me + j, n)))
-    stats, q = spread(1, stats, slots_s, groups, row, lambda j: (lax.rem(row + j, groups), me))
-    stat_ref[...] = jnp.concatenate([q, stats[1:]], axis=0)
+    if one_level:
+        mine = row * n + me
+
+        def other(j):
+            there = lax.rem(mine + j, n * groups)
+            return lax.div(there, n), lax.rem(there, n)
+
+        stats, q = spread(0, stats, slots_m, n * groups, mine, other)
+    else:
+        stats, q = spread(0, stats, slots_m, n, me, lambda j: (row, lax.rem(me + j, n)))
+        stats, q = spread(
+            1, stats, slots_s, groups, row, lambda j: (lax.rem(row + j, groups), me)
+        )
     scale = 1.0 / jnp.sqrt(stats[2 + nb : 3 + nb] / cells + 1e-6)
-    for s in range(sectors):
-        for p in range(size_p):
-            cols = slice(p * blk, (p + 1) * blk)
-            corr_ref[s, :, cols] = (hpsi_ref[s, :, cols] - q * corr_ref[s, :, cols]) * scale
+    stat_ref[...] = jnp.concatenate([q, scale, stats[2:]], axis=0)
     for copy in list(far.values()) + list(near.values()) + list(relay.values()):
         copy.wait_send()
     for copy in list(swaps.values()) + list(sends.values()):
         copy.wait_send()
+
+
+def out_kernel(h_ref, x_ref, stat_ref, hpsi_hbm, corr_hbm, ritz_ref, row_ref, corr, sem):
+    sectors, rows, width = h_ref.shape
+    blk = stat_ref.shape[1]
+    nb = row_ref.shape[1]
+    copies = [pltpu.make_async_copy(h_ref, hpsi_hbm, sem.at[sectors])]
+    copies[0].start()
+    q, scale = stat_ref[0:1, :], stat_ref[1:2, :]
+    for s in range(sectors):
+        for p in range(width // blk):
+            cols = slice(p * blk, (p + 1) * blk)
+            corr[s, :, cols] = (h_ref[s, :, cols] - q * x_ref[s, :, cols]) * scale
+        copies.append(pltpu.make_async_copy(corr.at[s], corr_hbm.at[s], sem.at[s]))
+        copies[-1].start()
+    ritz_ref[...] = q[:, :1]
+    lane = lax.broadcasted_iota(I32, (1, blk), 1)
+    line = jnp.zeros((1, blk), F32)
+    for j in range(nb):
+        line = jnp.where(lane == j, stat_ref[2 + j : 3 + j, :], line)
+    row_ref[...] = line[:, :nb]
+    for copy in copies:
+        copy.wait()
+
+
+def write_out(hpsi, x, stats, nb):
+    vmem = pl.BlockSpec(memory_space=pltpu.VMEM)
+    far = pl.BlockSpec(memory_space=pl.ANY)
+    like = jax.ShapeDtypeStruct(hpsi.shape, F32)
+    hpsi, correction, ritz, line = pl.pallas_call(
+        out_kernel,
+        out_shape=(
+            like,
+            like,
+            jax.ShapeDtypeStruct((1, 1), F32),
+            jax.ShapeDtypeStruct((1, nb), F32),
+        ),
+        in_specs=[vmem, vmem, vmem],
+        out_specs=(far, far, vmem, vmem),
+        scratch_shapes=[
+            pltpu.VMEM(hpsi.shape, F32),
+            pltpu.SemaphoreType.DMA((hpsi.shape[0] + 1,)),
+        ],
+        compiler_params=pltpu.CompilerParams(vmem_limit_bytes=4 * 2**20),
+        name="write_out",
+    )(hpsi, x, stats)
+    return (hpsi, correction, ritz.reshape(()), line.reshape(nb))
 
 
 def body(n, groups, psi, left_env, right_env, term_op, ops, energy, charge, block_dims, basis):
@@ -474,26 +534,23 @@
     wide = size_p * SUB
     smem = pl.BlockSpec(memory_space=pltpu.SMEM)
     vmem = pl.BlockSpec(memory_space=pltpu.VMEM)
-    far = pl.BlockSpec(memory_space=pl.ANY)
+    held = pl.BlockSpec(memory_space=pltpu.HBM)
     dma = pltpu.SemaphoreType.DMA
-    like = jax.ShapeDtypeStruct(psi.shape, F32)
+    like = pltpu.VMEM(psi.shape, F32)
     hops = max(chips - 1, 1)
-    hpsi, correction, stats = pl.pallas_call(
+    hpsi, x, stats = pl.pallas_call(
         functools.partial(kernel, n, groups, cells, pairs),
-        out_shape=(like, like, jax.ShapeDtypeStruct((8, blk), F32)),
-        in_specs=[smem, smem, smem, smem, vmem, far, far, far, far],
+        out_shape=(like, like, pltpu.VMEM((8, blk), F32)),
+        in_specs=[smem, smem, smem, smem, vmem, held, held, held, held],
         out_specs=(vmem, vmem, vmem),
         scratch_shapes=[
             pltpu.VMEM((sectors, CHUNKS, n, rows, cw), BF16),
             pltpu.VMEM((width, blk), BF16),
-            pltpu.VMEM(left_env.shape, BF16),
-            pltpu.VMEM(right_env.shape, BF16),
             pltpu.VMEM((sectors, blk, terms * blk), BF16),
             pltpu.VMEM((sectors, terms + 1, blk, blk), BF16),
             pltpu.VMEM((terms, blk, width), BF16),
             pltpu.VMEM((pairs + 1, size_p, blk, blk), F32),
             pltpu.VMEM((wide, 2 * op_count * wide), BF16),
-            pltpu.VMEM((size_p, blk, blk), F32),
             pltpu.VMEM((sectors, size_p, blk, blk), F32),
             pltpu.VMEM((chips, sectors, PARTS, pn, rows, blk), F32),
             pltpu.VMEM((hops, sectors, PARTS, pn * rows, blk), BF16),
@@ -501,7 +558,7 @@
             pltpu.VMEM(basis.shape, F32),
             pltpu.VMEM((8, 128), I32),
             pltpu.SMEM((8, 128), I32),
-            pltpu.VMEM((n, 8, blk), F32),
+            pltpu.VMEM((n * groups if n * groups <= FLAT else n, 8, blk), F32),
             pltpu.VMEM((groups, 8, blk), F32),
             pltpu.VMEM((2, 8, blk), F32),
             dma((sectors, CHUNKS)),
@@ -520,11 +577,11 @@
             dma((2,)),
         ],
         compiler_params=pltpu.CompilerParams(
-            collective_id=0, has_side_effects=True, vmem_limit_bytes=61 * 2**20
+            collective_id=0, has_side_effects=True, vmem_limit_bytes=56 * 2**20
         ),
         name="step",
     )(block_dims, charge, energy, term_op, ops, psi, left_env, right_env, basis)
-    return (hpsi, correction, stats[0, 0], stats[2 : 2 + nb, 0])
+    return write_out(hpsi, x, stats, nb)
 
 
 def solution(mesh):

time: 61.3 us -> 50.8 us (0.83)
  local copies, waits for them, and re-layouts: 6.23 us -> 0 us
  Pallas kernels: 54 us -> 49.9 us
    pallas_call x1, Pallas kernels: 54 us -> 48.4 us  [body(): pl.pallas_call(functools.partial(kernel, n, groups, cells, pairs), out_sh...]
    unnamed x2 -> x0, local copies, waits for them, and re-layouts: 3.74 us -> none
    slice x2 -> x0, local copies, waits for them, and re-layouts: 2.48 us -> none  [body(): return (hpsi, correction, stats[0, 0], stats[2:2 + nb, 0])]
    pallas_call x0 -> x1, Pallas kernels: none -> 1.5 us  [write_out(): pl.pallas_call(out_kernel, out_shape=(like, like, jax.ShapeDtypeStruct((1...]
where the time goes in v2:
time: 50.8 us; the launch traced here: 50.6 us
  Pallas kernels  49.9 us (98%)
  between operations  0.64 us (1%)
    pallas_call x1, Pallas kernels, body(): pl.pallas_call(functools.partial(kernel, n, groups, cells, pairs), out_sh...  48.4 us
    pallas_call x1, Pallas kernels, write_out(): pl.pallas_call(out_kernel, out_shape=(like, like, jax.ShapeDtypeStruct((1...  1.5 us

profile of v2, /device:TPU:0, one launch (start us, length us, event | category | flops | bytes accessed | tf_op | source)
XLA Modules:
  0.0 50.6 jit_solution(2693695281818150746)
XLA Ops:
  0.6 48.4 %step.1 = (f32[2,32,2048]{2,1,0:T(8,128)S(1)}, f32[2,32,2048]{2,1,0:T(8,128)S(1)}, f32[8,128]{1,0:T(8,128)S(1)}) custom-call(s32[2,2]{1,0:T(2,128)} %dims_ref.1, s32[2]{0:T(128)} %charge_ref.1, f32[16]{0:T(128)} %energy_ref.1, s32[32]{0:T(128)} %op_ref.1, bf16[8,16,16]{2,1,0:T(8,128)(2,1)} %ops_ref.1, bf16[2,32,2048]{2,1,0:T(8,128)(2,1)} %psi_hbm.1, ...), custom_call_target="tpu_custom_call" | custom-call | tf_op jit(solution)/shard_map/step/pallas_call | solution.py:541
  49.1 1.5 %write_out.1 = (f32[2,32,2048]{2,1,0:T(8,128)}, f32[2,32,2048]{2,1,0:T(8,128)}, f32[1,1]{1,0:T(1,128)}, f32[1,3]{1,0:T(1,128)}) custom-call(f32[2,32,2048]{2,1,0:T(8,128)S(1)} %get-tuple-element.11.h_ref, f32[2,32,2048]{2,1,0:T(8,128)S(1)} %get-tuple-element.12.x_ref, f32[8,128]{1,0:T(8,128)S(1)} %get-tuple-element.13.stat_ref), custom_call_target="tpu_custom_call" | custom-call | tf_op jit(solution)/shard_map/write_out/pallas_call | solution.py:504
